TPU v7x, 32 devices: a whole 2x2x4 slice. The times are simulated.
32 devices in a mesh: off: 4 (over y, x), img: 8 (over z, core).
Axes of the slice: x: 2, y: 2, z: 4, core: 2. Of those that a mesh axis runs over, the one named last changes fastest.
Arguments:
- traces: bfloat16 [1024, 3072], P(('off', 'img')), may hold values from -6 to 6
- offset_bins: int32 [1024], P(('off', 'img')), may hold values from 0 to 3, as said below
- class_slots: int32 [1024], P(('off', 'img')), may hold values from 0 to 7, as said below
- weights: bfloat16 [4, 4096, 256], P('off', 'img'), may hold values from -0.375 to 0.375
- band_start: int32 [4, 32], P('off', 'img'), may hold values from 0 to 1536
- smoothing: int32 [4, 32], P('off', 'img'), may hold values from 0 to 1
Outputs:
- migrated: bfloat16 [4, 4096, 1536], P('off', 'img')
Inputs may be any that keep to these rules, and one draw needn't show every extreme that they name: `offset_bins`: in each aligned block of 32 traces every class is named by exactly 8 traces. Within each aligned block of 32 traces the pairs (offset_bins, class_slots) are all distinct.
All inputs are finite; a program needn't handle non-finite values.
Results may differ from a plain program's by a relative error of at most 0.005.
Values may be sent and summed in bfloat16 or wider, within the bound.
A program may use at most 128 MiB of HBM per device.

v0:
```python
import jax
import jax.numpy as jnp
from jax import lax
from jax.sharding import PartitionSpec as P

NT = 1536
CB = 128


def filtered_levels(samples):
    values = samples.astype(jnp.float32)
    edges = [(0, 0)] * (values.ndim - 1)
    padded = jnp.pad(values, edges + [(1, 1)])
    boosted = values - 0.5 * (padded[..., :-2] + padded[..., 2:])
    widened = jnp.pad(boosted, edges + [(2, 2)])
    smoothed = (
        3.0 * boosted
        + 2.0 * (widened[..., 1:-3] + widened[..., 3:-1])
        + widened[..., :-4]
        + widened[..., 4:]
    ) / 9.0
    return jnp.stack([boosted, smoothed]).astype(jnp.bfloat16)


def migrate_rows(summed, shard_rows, weight_rows, band_rows, smooth_rows):
    row_count = shard_rows.shape[1]

    def segment(level_index, offset):
        return lax.dynamic_slice(shard_rows, (level_index, 0, offset), (1, row_count, NT))[0]

    segments = jax.vmap(segment)(smooth_rows, band_rows)
    blocks = band_rows.shape[0]
    columns = weight_rows
    columns = columns.reshape(blocks, CB, row_count)
    update = jnp.einsum("bcr,brt->bct", columns, segments, preferred_element_type=jnp.float32)
    return update.reshape(summed.shape)


def per_device(traces, offset_bins, class_slots, weights, band_start, smoothing):
    tr_count = traces.shape[0]
    per_class = tr_count // lax.axis_size("off")
    targets = offset_bins * per_class + class_slots
    weight_rows = weights[0]
    band_rows = band_start[0]
    smooth_rows = smoothing[0]
    initial = jnp.zeros((weight_rows.shape[0], NT), jnp.float32)
    levels = filtered_levels(traces)
    ordered = jnp.zeros_like(levels).at[:, targets].set(levels)
    regrouped = lax.all_to_all(ordered, "off", split_axis=1, concat_axis=1, tiled=True)
    summed = migrate_rows(
        initial,
        lax.all_gather(regrouped, "img", axis=1, tiled=True),
        weight_rows,
        band_rows,
        smooth_rows,
    )
    return summed.astype(jnp.bfloat16)[None]


def solution(mesh):
    in_specs = (
        P(("off", "img"), None),
        P(("off", "img")),
        P(("off", "img")),
        P("off", "img", None),
        P("off", "img"),
        P("off", "img"),
    )
    out_specs = P("off", "img", None)
    return jax.shard_map(
        per_device, mesh=mesh, in_specs=in_specs, out_specs=out_specs, check_vma=False
    )
```

profile of v0, /device:TPU:0, one launch (start us, length us, event | category | flops | bytes accessed | tf_op | source)
XLA Modules:
  0.0 86.1 jit_solution(13531859520118436541)
XLA Ops:
  6.5 0.0 copy-start
  6.5 0.0 copy-start.4
  6.5 0.0 copy-start.3
  6.5 0.0 copy-start.1
  6.5 0.0 copy-start.2
  6.5 0.0 all-gather.2.cloned.1.call-start
  6.6 1.0 %convert_element_type.24 = f32[32,3072]{1,0:T(8,128)S(1)} convert(bf16[32,3072]{1,0:T(8,128)(2,1)} %param.6) | non-fusion elementwise | flops 98304 | bytes 589824 | tf_op jit(solution)/shard_map/convert_element_type | solution.py:11
  7.6 0.3 convert_bitcast_fusion
  7.9 0.5 fusion.8
  8.4 0.4 copy.10
  8.8 0.0 copy-done.4
  8.8 0.0 copy-done.3
  8.8 0.2 broadcast_in_dim.4
  9.1 1.5 %scatter_fusion = bf16[2,32,3072]{2,0,1:T(2,128)(2,1)S(1)} fusion(bf16[2,32,3072]{2,0,1:T(2,128)(2,1)S(1)} %broadcast_in_dim.4, s32[32]{0:T(128)S(1)} %compare_select_fusion.2, bf16[32,2,3072]{2,1,0:T(2,128)(2,1)S(1)} %copy.10), kind=kCustom, calls=%fused_computation | custom fusion | bytes 1179776 | tf_op jit(solution)/shard_map/scatter | solution.py:48
  10.6 12.2 %all_to_all.5 = bf16[2,32,3072]{2,0,1:T(2,128)(2,1)} all-to-all(bf16[2,32,3072]{2,0,1:T(2,128)(2,1)S(1)} %scatter_fusion), channel_id=1, replica_groups=mesh['off'=4,'img'=8] {'off'}, dimensions={1} | all-to-all | bytes 786432 | tf_op jit(solution)/shard_map/all_to_all | solution.py:49
  22.8 0.0 all-gather.2.cloned.1.call-update
  22.8 0.0 copy-done.1
  22.8 0.0 copy-done.2
  22.9 0.1 copy.12
  23.0 38.0 %all-gather.2.cloned.1.call-done = bf16[2,256,3072]{2,0,1:T(2,128)(2,1)} async-done(((bf16[2,32,3072]{2,0,1:T(2,128)(2,1)}), bf16[2,256,3072]{2,0,1:T(2,128)(2,1)}) %all-gather.2.cloned.1.call-update) | async-done | bytes 3145744 | tf_op jit(solution)/shard_map/all_gather | solution.py:52
  61.0 2.7 %copy.11 = bf16[2,256,3072]{2,1,0:T(8,128)(2,1)S(1)} copy(bf16[2,256,3072]{2,0,1:T(2,128)(2,1)} %all-gather.2.cloned.1.call-done) | data formatting | bytes 6291456
  63.6 12.0 %while.1 = (s32[]{:T(128)}, bf16[2,256,3072]{2,1,0:T(8,128)(2,1)S(1)}, s32[4,3]{1,0:T(4,128)S(1)}, bf16[4,1,256,1536]{3,2,1,0:T(8,128)(2,1)}, s32[]{:T(128)}) while((s32[]{:T(128)}, bf16[2,256,3072]{2,1,0:T(8,128)(2,1)S(1)}, s32[4,3]{1,0:T(4,128)S(1)}, bf16[4,1,256,1536]{3,2,1,0:T(8,128)(2,1)}, s32[]{:T(128)}) %tuple.23), condition=%wide.while_cond, body=%wide.while_body.sunk | while | flops 2 | bytes 1574505 | solution.py:29
  63.7 0.6 fusion.13
  64.3 2.4 %bitcast_dynamic-update-slice_fusion.2 = bf16[4,1,256,1536]{3,2,1,0:T(8,128)(2,1)} fusion(bf16[4,1,256,1536]{3,2,1,0:T(8,128)(2,1)} %get-tuple-element.72, s32[]{:T(128)} %get-tuple-element.69, bf16[2,256,3072]{2,1,0:T(8,128)(2,1)S(1)} %get-tuple-element.75, s32[]{:T(128)} %bitcast.28, s32[]{:T(128)} %bitcast.29), kind=kLoop, calls=%fused_computation.1.clone.1 | loop fusion | bytes 1574400 | tf_op jit(solution)/shard_map/vmap()/gather
  66.6 0.6 fusion.13
  67.2 2.4 %bitcast_dynamic-update-slice_fusion.2 = bf16[4,1,256,1536]{3,2,1,0:T(8,128)(2,1)} fusion(bf16[4,1,256,1536]{3,2,1,0:T(8,128)(2,1)} %get-tuple-element.72, s32[]{:T(128)} %get-tuple-element.69, bf16[2,256,3072]{2,1,0:T(8,128)(2,1)S(1)} %get-tuple-element.75, s32[]{:T(128)} %bitcast.28, s32[]{:T(128)} %bitcast.29), kind=kLoop, calls=%fused_computation.1.clone.1 | loop fusion | bytes 1574400 | tf_op jit(solution)/shard_map/vmap()/gather
  69.7 0.6 fusion.13
  70.2 2.4 %bitcast_dynamic-update-slice_fusion.2 = bf16[4,1,256,1536]{3,2,1,0:T(8,128)(2,1)} fusion(bf16[4,1,256,1536]{3,2,1,0:T(8,128)(2,1)} %get-tuple-element.72, s32[]{:T(128)} %get-tuple-element.69, bf16[2,256,3072]{2,1,0:T(8,128)(2,1)S(1)} %get-tuple-element.75, s32[]{:T(128)} %bitcast.28, s32[]{:T(128)} %bitcast.29), kind=kLoop, calls=%fused_computation.1.clone.1 | loop fusion | bytes 1574400 | tf_op jit(solution)/shard_map/vmap()/gather
  72.6 0.6 fusion.13
  73.2 2.4 %bitcast_dynamic-update-slice_fusion.2 = bf16[4,1,256,1536]{3,2,1,0:T(8,128)(2,1)} fusion(bf16[4,1,256,1536]{3,2,1,0:T(8,128)(2,1)} %get-tuple-element.72, s32[]{:T(128)} %get-tuple-element.69, bf16[2,256,3072]{2,1,0:T(8,128)(2,1)S(1)} %get-tuple-element.75, s32[]{:T(128)} %bitcast.28, s32[]{:T(128)} %bitcast.29), kind=kLoop, calls=%fused_computation.1.clone.1 | loop fusion | bytes 1574400 | tf_op jit(solution)/shard_map/vmap()/gather
  75.6 0.0 copy-done
  75.6 3.6 %fusion.2 = bf16[4,1536,128]{1,2,0:T(8,128)(2,1)} fusion(bf16[4,128,256]{2,1,0:T(8,128)(2,1)S(1)} %bitcast.30, bf16[4,1,256,1536]{3,2,1,0:T(8,128)(2,1)} %get-tuple-element.12), kind=kOutput, calls=%fused_computation.5 | convolution fusion | flops 403439616 | bytes 4980736 | tf_op jit(solution)/shard_map/bcr,brt->bct/dot_general | solution.py:35
  (10 shorter events, 0.1 us)
Async XLA Ops:
  6.5 69.1 %copy-start = (bf16[1,512,256]{2,1,0:T(8,128)(2,1)S(1)}, bf16[1,512,256]{2,1,0:T(8,128)(2,1)}, u32[]{:S(2)}) copy-start(bf16[1,512,256]{2,1,0:T(8,128)(2,1)} %param.9) | copy-start | bytes 786436
  6.5 2.3 %copy-start.4 = (s32[32]{0:T(128)S(1)}, s32[32]{0:T(128)}, u32[]{:S(2)}) copy-start(s32[32]{0:T(128)} %param.7) | copy-start | bytes 388
  6.5 2.3 %copy-start.3 = (s32[32]{0:T(128)S(1)}, s32[32]{0:T(128)}, u32[]{:S(2)}) copy-start(s32[32]{0:T(128)} %param.8) | copy-start | bytes 388
  6.5 16.3 %copy-start.1 = (s32[1,4]{1,0:T(1,128)S(1)}, s32[1,4]{1,0:T(1,128)}, u32[]{:S(2)}) copy-start(s32[1,4]{1,0:T(1,128)} %param.10) | copy-start | bytes 52
  6.5 16.3 %copy-start.2 = (s32[1,4]{1,0:T(1,128)S(1)}, s32[1,4]{1,0:T(1,128)}, u32[]{:S(2)}) copy-start(s32[1,4]{1,0:T(1,128)} %param.11) | copy-start | bytes 52
  6.5 54.4 %all-gather.2.cloned.1.call-start = ((), (), s32[]{:S(2)}) async-start(), calls=%async_computation.1 | async-start | bytes 3538944 | tf_op jit(solution)/shard_map/all_gather | solution.py:52
Sparse Core Ops, SparseCore 0:
  22.9 37.9 all-gather.1
where the time goes:
time: 86.4 us; the launch traced here: 86.1 us
  waiting for transfers between devices  38 us (44%)
  local copies, waits for them, and re-layouts  16.9 us (20%)
  between operations  13.5 us (16%)
  blocking collectives  12.2 us (14%)
  matrix products  3.63 us (4%)
  other arithmetic  1.81 us (2%)
    all_gather x1, waiting for transfers between devices, per_device(): lax.all_gather(regrouped, 'img', axis=1, tiled=True)  38 us
    all_to_all x1, blocking collectives, per_device(): lax.all_to_all(ordered, 'off', split_axis=1, concat_axis=1, tiled=True)  12.2 us
    gather x12, local copies, waits for them, and re-layouts  11.9 us
    dot_general x1, matrix products, migrate_rows(): jnp.einsum('bcr,brt->bct', columns, segments, preferred_element_type=jnp....  3.63 us
    unnamed x12, local copies, waits for them, and re-layouts  2.78 us
  transfers between devices with their start and end apart: 1, of which 1 were waited for; matrix products, arithmetic and copies ran while one was open for 0% of the time, Pallas kernels for 0%

commit v1 on v0

v1 whole, which is shorter than its diff:
```python
import functools

import jax
import jax.numpy as jnp
from jax import lax
from jax.experimental import pallas as pl
from jax.experimental.pallas import tpu as pltpu
from jax.sharding import PartitionSpec as P

NT = 1536
CB = 128
MESH = pl.DeviceIdType.MESH


def gather_kernel(n_off, n_img, traces_ref, bins_ref, slots_ref, buf, send, xy_sem, up_sem, down_sem, sib_sem, recv_sem):
    o = lax.axis_index("off")
    i = lax.axis_index("img")
    rows = traces_ref.shape[0]
    per = rows // n_off
    lines = n_img // 2
    z = i // 2
    core = i % 2
    sibling = z * 2 + 1 - core
    has_up = z < lines - 1
    has_down = z > 0

    barrier = pltpu.get_barrier_semaphore()
    for step in range(1, n_off):
        pl.semaphore_signal(barrier, inc=1, device_id=((o + step) % n_off, i), device_id_type=MESH)
    pl.semaphore_signal(barrier, inc=1, device_id=(o, sibling), device_id_type=MESH)

    @pl.when(has_up)
    def _():
        pl.semaphore_signal(barrier, inc=1, device_id=(o, i + 2), device_id_type=MESH)

    @pl.when(has_down)
    def _():
        pl.semaphore_signal(barrier, inc=1, device_id=(o, i - 2), device_id_type=MESH)

    targets = bins_ref[...] * per + slots_ref[...]
    onehot = jnp.where(lax.broadcasted_iota(jnp.int32, (rows, rows), 0) == targets, 1.0, 0.0).astype(jnp.bfloat16)
    ordered = jnp.dot(onehot, traces_ref[...], preferred_element_type=jnp.float32)
    for p in range(n_off):
        send[p] = ordered[p * per:(p + 1) * per].astype(jnp.bfloat16)
    buf[i, o] = send[o]

    pl.semaphore_wait(barrier, n_off + jnp.where(has_up, 1, 0) + jnp.where(has_down, 1, 0))

    def xy_copy(step):
        p = (o + step) % n_off
        return pltpu.make_async_remote_copy(
            src_ref=send.at[p], dst_ref=buf.at[i, o], send_sem=xy_sem.at[step], recv_sem=recv_sem.at[i, o],
            device_id=(p, i), device_id_type=MESH)

    def chunk_copy(j, q, sems, target):
        return pltpu.make_async_remote_copy(
            src_ref=buf.at[j, q], dst_ref=buf.at[j, q], send_sem=sems.at[j, q], recv_sem=recv_sem.at[j, q],
            device_id=(o, target), device_id_type=MESH)

    def arrived(j, q):
        pltpu.make_async_remote_copy(
            src_ref=buf.at[j, q], dst_ref=buf.at[j, q], send_sem=sib_sem.at[j, q], recv_sem=recv_sem.at[j, q],
            device_id=(o, sibling), device_id_type=MESH).wait_recv()

    for step in range(1, n_off):
        xy_copy(step).start()

    for step in range(n_off):
        q = (o - step + n_off) % n_off
        if step > 0:
            arrived(i, q)

        @pl.when(has_up)
        def _():
            chunk_copy(i, q, up_sem, i + 2).start()

        @pl.when(has_down)
        def _():
            chunk_copy(i, q, down_sem, i - 2).start()

        chunk_copy(i, q, sib_sem, sibling).start()

    for d in range(1, lines):
        below = i - 2 * d
        above = i + 2 * d

        def one_chunk(step, carry):
            q = (o - step + n_off) % n_off

            @pl.when(z >= d)
            def _():
                arrived(below, q)

                @pl.when(has_up)
                def _():
                    chunk_copy(below, q, up_sem, i + 2).start()

                chunk_copy(below, q, sib_sem, sibling).start()

            @pl.when(z + d < lines)
            def _():
                arrived(above, q)

                @pl.when(has_down)
                def _():
                    chunk_copy(above, q, down_sem, i - 2).start()

                chunk_copy(above, q, sib_sem, sibling).start()

            return carry

        lax.fori_loop(0, n_off, one_chunk, 0)

    for w in range(lines):

        def last(q, carry):
            arrived(2 * w + 1 - core, q)
            mine = 2 * w + core
            chunk_copy(mine, q, sib_sem, sibling).wait_send()

            @pl.when(jnp.logical_and(has_up, w <= z))
            def _():
                chunk_copy(mine, q, up_sem, i + 2).wait_send()

            @pl.when(jnp.logical_and(has_down, w >= z))
            def _():
                chunk_copy(mine, q, down_sem, i - 2).wait_send()

            return carry

        lax.fori_loop(0, n_off, last, 0)

    for step in range(1, n_off):
        xy_copy(step).wait_send()


def gather_rows(traces, offset_bins, class_slots):
    n_off = lax.axis_size("off")
    n_img = lax.axis_size("img")
    rows, samples = traces.shape
    per = rows // n_off
    vmem = pl.BlockSpec(memory_space=pltpu.VMEM)
    return pl.pallas_call(
        functools.partial(gather_kernel, n_off, n_img),
        out_shape=jax.ShapeDtypeStruct((n_img, n_off, per, samples), jnp.bfloat16),
        in_specs=[vmem] * 3,
        out_specs=vmem,
        scratch_shapes=[
            pltpu.VMEM((n_off, per, samples), jnp.bfloat16),
            pltpu.SemaphoreType.DMA((n_off,)),
            pltpu.SemaphoreType.DMA((n_img, n_off)),
            pltpu.SemaphoreType.DMA((n_img, n_off)),
            pltpu.SemaphoreType.DMA((n_img, n_off)),
            pltpu.SemaphoreType.DMA((n_img, n_off)),
        ],
        compiler_params=pltpu.CompilerParams(
            collective_id=0, has_side_effects=True, vmem_limit_bytes=48 * 1024 * 1024),
        name="gather_rows",
    )(traces, offset_bins.reshape(1, rows), class_slots.reshape(1, rows))


def migrate_kernel(band_ref, smooth_ref, raw_ref, weights_ref, out_ref, levels):
    rows, samples = raw_ref.shape
    block = pl.program_id(0)

    @pl.when(block == 0)
    def _():
        gap = jnp.zeros((16, 128), jnp.float32)
        width = samples + 128

        def filter_rows(group, carry):
            at = pl.ds(pl.multiple_of(group * 16, 16), 16)
            values = jnp.concatenate([raw_ref[at, :].astype(jnp.float32), gap], axis=1)
            boosted = values - 0.5 * (pltpu.roll(values, 1, 1) + pltpu.roll(values, width - 1, 1))
            boosted = boosted[:, :samples]
            wide = jnp.concatenate([boosted, gap], axis=1)
            smoothed = (
                3.0 * wide
                + 2.0 * (pltpu.roll(wide, 1, 1) + pltpu.roll(wide, width - 1, 1))
                + pltpu.roll(wide, 2, 1)
                + pltpu.roll(wide, width - 2, 1)
            ) / 9.0
            levels[0, at, :] = boosted.astype(jnp.bfloat16)
            levels[1, at, :] = smoothed[:, :samples].astype(jnp.bfloat16)
            return carry

        lax.fori_loop(0, rows // 16, filter_rows, 0)

    start = band_ref[block]
    span = NT + 128
    base = jnp.minimum(start // 128, (samples - span) // 128) * 128
    shift = start - base
    segment = levels[smooth_ref[block], :, pl.ds(pl.multiple_of(base, 128), span)]
    product = jnp.dot(weights_ref[...], segment, preferred_element_type=jnp.float32)
    turned = pltpu.roll(product, lax.rem(span - shift, span), 1)
    out_ref[...] = turned[:, :NT].astype(jnp.bfloat16)


def migrate(raw, weight_rows, band_rows, smooth_rows):
    rows, samples = raw.shape
    columns = weight_rows.shape[0]
    return pl.pallas_call(
        migrate_kernel,
        out_shape=jax.ShapeDtypeStruct((columns, NT), jnp.bfloat16),
        grid_spec=pltpu.PrefetchScalarGridSpec(
            num_scalar_prefetch=2,
            grid=(columns // CB,),
            in_specs=[
                pl.BlockSpec((rows, samples), lambda b, *_: (0, 0)),
                pl.BlockSpec((CB, rows), lambda b, *_: (b, 0)),
            ],
            out_specs=pl.BlockSpec((CB, NT), lambda b, *_: (b, 0)),
            scratch_shapes=[pltpu.VMEM((2, rows, samples), jnp.bfloat16)],
        ),
        compiler_params=pltpu.CompilerParams(vmem_limit_bytes=48 * 1024 * 1024),
        name="migrate",
    )(band_rows, smooth_rows, raw, weight_rows)


def per_device(traces, offset_bins, class_slots, weights, band_start, smoothing):
    raw = gather_rows(traces, offset_bins, class_slots)
    raw = raw.reshape(-1, traces.shape[1])
    return migrate(raw, weights[0], band_start[0], smoothing[0])[None]


def solution(mesh):
    in_specs = (
        P(("off", "img"), None),
        P(("off", "img")),
        P(("off", "img")),
        P("off", "img", None),
        P("off", "img"),
        P("off", "img"),
    )
    out_specs = P("off", "img", None)
    return jax.shard_map(
        per_device, mesh=mesh, in_specs=in_specs, out_specs=out_specs, check_vma=False
    )
```

time: 86.4 us -> 34.5 us (0.40)
  waiting for transfers between devices: 38 us -> 0 us
  Pallas kernels: 0 us -> 32 us
  local copies, waits for them, and re-layouts: 16.9 us -> 2.29 us
  between operations: 13.5 us -> 0.04 us
  blocking collectives: 12.2 us -> 0 us
  matrix products: 3.63 us -> 0 us
  other arithmetic: 1.81 us -> 0 us
    all_gather x1 -> x0, waiting for transfers between devices: 38 us -> none  [per_device(): lax.all_gather(regrouped, 'img', axis=1, tiled=True)]
    pallas_call x0 -> x2, Pallas kernels: none -> 32 us  [the longest x1 22.3 us: gather_rows(): pl.pallas_call(functools.partial(gather_kernel, n_off, n_img), out_shape=...]
    all_to_all x1 -> x0, blocking collectives: 12.2 us -> none  [per_device(): lax.all_to_all(ordered, 'off', split_axis=1, concat_axis=1, tiled=True)]
    gather x12 -> x0, local copies, waits for them, and re-layouts: 11.9 us -> none
    dot_general x1 -> x0, matrix products: 3.63 us -> none  [migrate_rows(): jnp.einsum('bcr,brt->bct', columns, segments, preferred_element_type=jnp....]
    scatter x1 -> x0, local copies, waits for them, and re-layouts: 1.54 us -> none  [per_device(): ordered = jnp.zeros_like(levels).at[:, targets].set(levels)]
    convert_element_type x1 -> x0, other arithmetic: 1 us -> none  [filtered_levels(): values = samples.astype(jnp.float32)]
  transfers between devices with their start and end apart: 1 -> 0, of which waited for: 1 -> 0; matrix products, arithmetic and copies ran while one was open for 0% -> 0% of each run, Pallas kernels for 0% -> 0%
where the time goes in v1:
time: 34.5 us; the launch traced here: 34.4 us
  Pallas kernels  32 us (93%)
  local copies, waits for them, and re-layouts  2.29 us (7%)
    pallas_call x1, Pallas kernels, gather_rows(): pl.pallas_call(functools.partial(gather_kernel, n_off, n_img), out_shape=...  22.3 us
    pallas_call x1, Pallas kernels, migrate(): pl.pallas_call(migrate_kernel, out_shape=jax.ShapeDtypeStruct((columns, N...  9.69 us
    unnamed x12, local copies, waits for them, and re-layouts  2.29 us

profile of v1, /device:TPU:0, one launch (start us, length us, event | category | flops | bytes accessed | tf_op | source)
XLA Modules:
  0.0 34.4 jit_solution(10893317915934294504)
XLA Ops:
  0.0 0.0 copy-start
  0.0 0.0 copy-start.1
  0.0 1.0 %copy-done.1 = bf16[32,3072]{1,0:T(8,128)(2,1)S(1)} copy-done((bf16[32,3072]{1,0:T(8,128)(2,1)S(1)}, bf16[32,3072]{1,0:T(8,128)(2,1)}, u32[]{:S(2)}) %copy-start.1) | copy-done | bytes 196632
  1.0 0.0 copy-start.2
  1.0 0.7 %copy-done.2 = s32[32]{0:T(128)S(1)} copy-done((s32[32]{0:T(128)S(1)}, s32[32]{0:T(128)}, u32[]{:S(2)}) %copy-start.2) | copy-done | bytes 152
  1.6 0.0 copy-start.3
  1.6 0.7 %copy-done.3 = s32[32]{0:T(128)S(1)} copy-done((s32[32]{0:T(128)S(1)}, s32[32]{0:T(128)}, u32[]{:S(2)}) %copy-start.3) | copy-done | bytes 152
  2.3 0.0 copy-start.4
  2.3 0.0 copy-start.5
  2.3 22.3 %gather_rows.1 = bf16[8,4,8,3072]{3,2,1,0:T(8,128)(2,1)S(1)} custom-call(bf16[32,3072]{1,0:T(8,128)(2,1)S(1)} %copy-done.1, s32[1,32]{1,0:T(1,128)S(1)} %bitcast.9, s32[1,32]{1,0:T(1,128)S(1)} %bitcast.10), custom_call_target="tpu_custom_call" | custom-call | tf_op jit(solution)/shard_map/gather_rows/pallas_call | solution.py:143
  24.6 0.0 copy-done
  24.6 0.0 copy-done.4
  24.7 0.0 copy-done.5
  24.7 9.7 %migrate.1 = bf16[512,1536]{1,0:T(8,128)(2,1)} custom-call(s32[4]{0:T(128)S(1)} %bitcast.11, s32[4]{0:T(128)S(1)} %bitcast.12, bf16[256,3072]{1,0:T(8,128)(2,1)S(1)} %bitcast.7, bf16[512,256]{1,0:T(8,128)(2,1)S(1)} %bitcast.8), custom_call_target="tpu_custom_call" | custom-call | tf_op jit(solution)/shard_map/migrate/pallas_call | solution.py:202
Async XLA Ops:
  0.0 24.6 %copy-start = (bf16[1,512,256]{2,1,0:T(8,128)(2,1)S(1)}, bf16[1,512,256]{2,1,0:T(8,128)(2,1)}, u32[]{:S(2)}) copy-start(bf16[1,512,256]{2,1,0:T(8,128)(2,1)} %param.9) | copy-start | bytes 786436
  0.0 1.0 %copy-start.1 = (bf16[32,3072]{1,0:T(8,128)(2,1)S(1)}, bf16[32,3072]{1,0:T(8,128)(2,1)}, u32[]{:S(2)}) copy-start(bf16[32,3072]{1,0:T(8,128)(2,1)} %traces_ref.1) | copy-start | bytes 589828
  1.0 0.7 %copy-start.2 = (s32[32]{0:T(128)S(1)}, s32[32]{0:T(128)}, u32[]{:S(2)}) copy-start(s32[32]{0:T(128)} %param.7) | copy-start | bytes 388
  1.6 0.7 %copy-start.3 = (s32[32]{0:T(128)S(1)}, s32[32]{0:T(128)}, u32[]{:S(2)}) copy-start(s32[32]{0:T(128)} %param.8) | copy-start | bytes 388
  2.3 22.4 %copy-start.4 = (s32[1,4]{1,0:T(1,128)S(1)}, s32[1,4]{1,0:T(1,128)}, u32[]{:S(2)}) copy-start(s32[1,4]{1,0:T(1,128)} %param.10) | copy-start | bytes 52
  2.3 22.4 %copy-start.5 = (s32[1,4]{1,0:T(1,128)S(1)}, s32[1,4]{1,0:T(1,128)}, u32[]{:S(2)}) copy-start(s32[1,4]{1,0:T(1,128)} %param.11) | copy-start | bytes 52

commit v2 on v1

v2 whole, which is shorter than its diff:
```python
import functools

import jax
import jax.numpy as jnp
from jax import lax
from jax.experimental import pallas as pl
from jax.experimental.pallas import tpu as pltpu
from jax.sharding import PartitionSpec as P

NT = 1536
CB = 128
MESH = pl.DeviceIdType.MESH


def gather_kernel(n_off, n_img, traces_hbm, bins_hbm, slots_hbm, out, traces_ref, bins_ref, slots_ref, buf, levels, send,
                  in_sem, xy_sem, up_sem, down_sem, sib_sem, recv_sem, out_sem):
    o = lax.axis_index("off")
    i = lax.axis_index("img")
    rows = traces_ref.shape[0]
    per = rows // n_off
    lines = n_img // 2
    z = i // 2
    core = i % 2
    sibling = z * 2 + 1 - core
    has_up = z < lines - 1
    has_down = z > 0

    inputs = [
        pltpu.make_async_copy(source, held, in_sem.at[n])
        for n, (source, held) in enumerate(
            [(traces_hbm, traces_ref), (bins_hbm, bins_ref), (slots_hbm, slots_ref)])
    ]
    for copy in inputs:
        copy.start()

    barrier = pltpu.get_barrier_semaphore()
    for step in range(1, n_off):
        pl.semaphore_signal(barrier, inc=1, device_id=((o + step) % n_off, i), device_id_type=MESH)
    pl.semaphore_signal(barrier, inc=1, device_id=(o, sibling), device_id_type=MESH)

    @pl.when(has_up)
    def _():
        pl.semaphore_signal(barrier, inc=1, device_id=(o, i + 2), device_id_type=MESH)

    @pl.when(has_down)
    def _():
        pl.semaphore_signal(barrier, inc=1, device_id=(o, i - 2), device_id_type=MESH)

    for copy in inputs:
        copy.wait()
    targets = bins_ref[...] * per + slots_ref[...]
    onehot = jnp.where(lax.broadcasted_iota(jnp.int32, (rows, rows), 0) == targets, 1.0, 0.0).astype(jnp.bfloat16)
    ordered = jnp.dot(onehot, traces_ref[...], preferred_element_type=jnp.float32)
    for p in range(n_off):
        send[p] = ordered[p * per:(p + 1) * per].astype(jnp.bfloat16)
    buf[i, o] = send[o]

    pl.semaphore_wait(barrier, n_off + jnp.where(has_up, 1, 0) + jnp.where(has_down, 1, 0))

    def xy_copy(step):
        p = (o + step) % n_off
        return pltpu.make_async_remote_copy(
            src_ref=send.at[p], dst_ref=buf.at[i, o], send_sem=xy_sem.at[step], recv_sem=recv_sem.at[i, o],
            device_id=(p, i), device_id_type=MESH)

    def chunk_copy(j, q, sems, target):
        return pltpu.make_async_remote_copy(
            src_ref=buf.at[j, q], dst_ref=buf.at[j, q], send_sem=sems.at[j, q], recv_sem=recv_sem.at[j, q],
            device_id=(o, target), device_id_type=MESH)

    def arrived(j, q):
        pltpu.make_async_remote_copy(
            src_ref=buf.at[j, q], dst_ref=buf.at[j, q], send_sem=sib_sem.at[j, q], recv_sem=recv_sem.at[j, q],
            device_id=(o, sibling), device_id_type=MESH).wait_recv()

    for step in range(1, n_off):
        xy_copy(step).start()

    def out_copy(j, q):
        return pltpu.make_async_copy(levels.at[:, j, q], out.at[:, j, q], out_sem.at[j, q])

    def filter_chunk(j, q):
        samples = buf.shape[3]
        width = samples + 128
        gap = jnp.zeros((per, 128), jnp.float32)
        values = jnp.concatenate([buf[j, q].astype(jnp.float32), gap], axis=1)
        boosted = values - 0.5 * (pltpu.roll(values, 1, 1) + pltpu.roll(values, width - 1, 1))
        boosted = boosted[:, :samples]
        wide = jnp.concatenate([boosted, gap], axis=1)
        smoothed = (
            3.0 * wide
            + 2.0 * (pltpu.roll(wide, 1, 1) + pltpu.roll(wide, width - 1, 1))
            + pltpu.roll(wide, 2, 1)
            + pltpu.roll(wide, width - 2, 1)
        ) / 9.0
        levels[0, j, q] = boosted.astype(jnp.bfloat16)
        levels[1, j, q] = smoothed[:, :samples].astype(jnp.bfloat16)
        out_copy(j, q).start()

    def first_chunk(step, carry):
        q = lax.rem(o - step + n_off, n_off)

        @pl.when(step > 0)
        def _():
            arrived(i, q)

        @pl.when(has_up)
        def _():
            chunk_copy(i, q, up_sem, i + 2).start()

        @pl.when(has_down)
        def _():
            chunk_copy(i, q, down_sem, i - 2).start()

        chunk_copy(i, q, sib_sem, sibling).start()
        filter_chunk(i, q)
        return carry

    lax.fori_loop(0, n_off, first_chunk, 0)

    def one_chunk(turn, carry):
        d = lax.div(turn, n_off) + 1
        q = lax.rem(o - lax.rem(turn, n_off) + n_off, n_off)
        below = i - 2 * d
        above = i + 2 * d
        from_below = z >= d
        from_above = z + d < lines

        @pl.when(from_below)
        def _():
            arrived(below, q)

            @pl.when(has_up)
            def _():
                chunk_copy(below, q, up_sem, i + 2).start()

            chunk_copy(below, q, sib_sem, sibling).start()

        @pl.when(from_above)
        def _():
            arrived(above, q)

            @pl.when(has_down)
            def _():
                chunk_copy(above, q, down_sem, i - 2).start()

            chunk_copy(above, q, sib_sem, sibling).start()

        @pl.when(from_below)
        def _():
            filter_chunk(below, q)

        @pl.when(from_above)
        def _():
            filter_chunk(above, q)

        near = d - 1

        @pl.when(z >= near)
        def _():
            arrived(sibling - 2 * near, q)
            filter_chunk(sibling - 2 * near, q)

        @pl.when(jnp.logical_and(near > 0, z + near < lines))
        def _():
            arrived(sibling + 2 * near, q)
            filter_chunk(sibling + 2 * near, q)

        return carry

    lax.fori_loop(0, lines * n_off, one_chunk, 0)

    for w in range(lines):

        def last(q, carry):
            mine = 2 * w + core
            out_copy(2 * w, q).wait()
            out_copy(2 * w + 1, q).wait()
            chunk_copy(mine, q, sib_sem, sibling).wait_send()

            @pl.when(jnp.logical_and(has_up, w <= z))
            def _():
                chunk_copy(mine, q, up_sem, i + 2).wait_send()

            @pl.when(jnp.logical_and(has_down, w >= z))
            def _():
                chunk_copy(mine, q, down_sem, i - 2).wait_send()

            return carry

        lax.fori_loop(0, n_off, last, 0)

    for step in range(1, n_off):
        xy_copy(step).wait_send()


def gather_levels(traces, offset_bins, class_slots):
    n_off = lax.axis_size("off")
    n_img = lax.axis_size("img")
    rows, samples = traces.shape
    per = rows // n_off
    hbm = pl.BlockSpec(memory_space=pl.ANY)
    return pl.pallas_call(
        functools.partial(gather_kernel, n_off, n_img),
        out_shape=jax.ShapeDtypeStruct((2, n_img, n_off, per, samples), jnp.bfloat16),
        in_specs=[hbm] * 3,
        out_specs=hbm,
        scratch_shapes=[
            pltpu.VMEM((rows, samples), jnp.bfloat16),
            pltpu.VMEM((1, rows), jnp.int32),
            pltpu.VMEM((1, rows), jnp.int32),
            pltpu.VMEM((n_img, n_off, per, samples), jnp.bfloat16),
            pltpu.VMEM((2, n_img, n_off, per, samples), jnp.bfloat16),
            pltpu.VMEM((n_off, per, samples), jnp.bfloat16),
            pltpu.SemaphoreType.DMA((3,)),
            pltpu.SemaphoreType.DMA((n_off,)),
            pltpu.SemaphoreType.DMA((n_img, n_off)),
            pltpu.SemaphoreType.DMA((n_img, n_off)),
            pltpu.SemaphoreType.DMA((n_img, n_off)),
            pltpu.SemaphoreType.DMA((n_img, n_off)),
            pltpu.SemaphoreType.DMA((n_img, n_off)),
        ],
        compiler_params=pltpu.CompilerParams(
            collective_id=0, has_side_effects=True, vmem_limit_bytes=56 * 1024 * 1024),
        name="gather_levels",
    )(traces, offset_bins.reshape(1, rows), class_slots.reshape(1, rows))


def migrate_kernel(band_ref, smooth_ref, levels, weights_ref, out_ref, segments, sems):
    samples = levels.shape[2]
    span = segments.shape[2]
    blocks = segments.shape[0]
    block = pl.program_id(0)

    def base_of(b):
        return jnp.minimum(lax.div(band_ref[b], 128), (samples - span) // 128) * 128

    def segment_copy(b):
        band = pl.ds(pl.multiple_of(base_of(b), 128), span)
        return pltpu.make_async_copy(levels.at[smooth_ref[b], :, band], segments.at[b], sems.at[b])

    @pl.when(block == 0)
    def _():
        for b in range(blocks):
            segment_copy(b).start()

    segment_copy(block).wait()
    shift = band_ref[block] - base_of(block)
    product = jnp.dot(weights_ref[...], segments[block], preferred_element_type=jnp.float32)
    turned = pltpu.roll(product, lax.rem(span - shift, span), 1)
    out_ref[...] = turned[:, :NT].astype(jnp.bfloat16)


def migrate(levels, weight_rows, band_rows, smooth_rows):
    rows = levels.shape[1]
    columns = weight_rows.shape[0]
    blocks = columns // CB
    return pl.pallas_call(
        migrate_kernel,
        out_shape=jax.ShapeDtypeStruct((columns, NT), jnp.bfloat16),
        grid_spec=pltpu.PrefetchScalarGridSpec(
            num_scalar_prefetch=2,
            grid=(blocks,),
            in_specs=[
                pl.BlockSpec(memory_space=pl.ANY),
                pl.BlockSpec((CB, rows), lambda b, *_: (b, 0)),
            ],
            out_specs=pl.BlockSpec((CB, NT), lambda b, *_: (b, 0)),
            scratch_shapes=[
                pltpu.VMEM((blocks, rows, NT + 128), jnp.bfloat16),
                pltpu.SemaphoreType.DMA((blocks,)),
            ],
        ),
        compiler_params=pltpu.CompilerParams(vmem_limit_bytes=48 * 1024 * 1024),
        name="migrate",
    )(band_rows, smooth_rows, levels, weight_rows)


def per_device(traces, offset_bins, class_slots, weights, band_start, smoothing):
    levels = gather_levels(traces, offset_bins, class_slots)
    levels = levels.reshape(2, -1, traces.shape[1])
    return migrate(levels, weights[0], band_start[0], smoothing[0])[None]


def solution(mesh):
    in_specs = (
        P(("off", "img"), None),
        P(("off", "img")),
        P(("off", "img")),
        P("off", "img", None),
        P("off", "img"),
        P("off", "img"),
    )
    out_specs = P("off", "img", None)
    return jax.shard_map(
        per_device, mesh=mesh, in_specs=in_specs, out_specs=out_specs, check_vma=False
    )
```

time: 34.5 us -> 30.8 us (0.89)
  Pallas kernels: 32 us -> 28.7 us
  local copies, waits for them, and re-layouts: 2.29 us -> 1.89 us
    pallas_call x1, Pallas kernels: 9.69 us -> 3.87 us  [migrate(): pl.pallas_call(migrate_kernel, out_shape=jax.ShapeDtypeStruct((columns, N...]
    pallas_call x1, Pallas kernels: 22.3 us -> 24.8 us  [gather_levels(): pl.pallas_call(functools.partial(gather_kernel, n_off, n_img), out_shape=...]
    unnamed x12 -> x8, local copies, waits for them, and re-layouts: 2.29 us -> 1.89 us
where the time goes in v2:
time: 30.8 us; the launch traced here: 30.6 us
  Pallas kernels  28.7 us (93%)
  local copies, waits for them, and re-layouts  1.89 us (6%)
    pallas_call x1, Pallas kernels, gather_levels(): pl.pallas_call(functools.partial(gather_kernel, n_off, n_img), out_shape=...  24.8 us
    pallas_call x1, Pallas kernels, migrate(): pl.pallas_call(migrate_kernel, out_shape=jax.ShapeDtypeStruct((columns, N...  3.87 us
    unnamed x8, local copies, waits for them, and re-layouts  1.89 us

profile of v2, /device:TPU:0, one launch (start us, length us, event | category | flops | bytes accessed | tf_op | source)
XLA Modules:
  0.0 30.6 jit_solution(14321272475059180588)
XLA Ops:
  0.0 0.0 copy-start.3
  0.0 0.0 copy-start.2
  0.0 0.0 copy-start.1
  0.0 24.8 %gather_levels.1 = bf16[2,8,4,8,3072]{4,3,2,1,0:T(8,128)(2,1)} custom-call(bf16[32,3072]{1,0:T(8,128)(2,1)} %traces_hbm.1, s32[1,32]{1,0:T(1,128)} %bitcast.11, s32[1,32]{1,0:T(1,128)} %bitcast.12), custom_call_target="tpu_custom_call" | custom-call | tf_op jit(solution)/shard_map/gather_levels/pallas_call | solution.py:203
  24.8 0.0 copy-done.3
  24.9 0.0 copy-done.2
  24.9 0.0 copy-done.1
  24.9 0.0 copy-start
  24.9 1.9 %copy-done = bf16[2,8,4,8,3072]{4,3,2,1,0:T(8,128)(2,1)S(1)} copy-done((bf16[2,8,4,8,3072]{4,3,2,1,0:T(8,128)(2,1)S(1)}, bf16[2,8,4,8,3072]{4,3,2,1,0:T(8,128)(2,1)}, u32[]{:S(2)}) %copy-start) | copy-done | bytes 3145752
  26.8 3.9 %migrate.1 = bf16[512,1536]{1,0:T(8,128)(2,1)} custom-call(s32[4]{0:T(128)S(1)} %bitcast.9, s32[4]{0:T(128)S(1)} %bitcast.10, bf16[2,256,3072]{2,1,0:T(8,128)(2,1)S(1)} %bitcast.7, bf16[512,256]{1,0:T(8,128)(2,1)S(1)} %bitcast.8), custom_call_target="tpu_custom_call" | custom-call | tf_op jit(solution)/shard_map/migrate/pallas_call | solution.py:258
Async XLA Ops:
  0.0 24.8 %copy-start.3 = (s32[1,4]{1,0:T(1,128)S(1)}, s32[1,4]{1,0:T(1,128)}, u32[]{:S(2)}) copy-start(s32[1,4]{1,0:T(1,128)} %param.11) | copy-start | bytes 52
  0.0 24.9 %copy-start.2 = (s32[1,4]{1,0:T(1,128)S(1)}, s32[1,4]{1,0:T(1,128)}, u32[]{:S(2)}) copy-start(s32[1,4]{1,0:T(1,128)} %param.10) | copy-start | bytes 52
  0.0 24.9 %copy-start.1 = (bf16[1,512,256]{2,1,0:T(8,128)(2,1)S(1)}, bf16[1,512,256]{2,1,0:T(8,128)(2,1)}, u32[]{:S(2)}) copy-start(bf16[1,512,256]{2,1,0:T(8,128)(2,1)} %param.9) | copy-start | bytes 786436
  24.9 1.9 %copy-start = (bf16[2,8,4,8,3072]{4,3,2,1,0:T(8,128)(2,1)S(1)}, bf16[2,8,4,8,3072]{4,3,2,1,0:T(8,128)(2,1)}, u32[]{:S(2)}) copy-start(bf16[2,8,4,8,3072]{4,3,2,1,0:T(8,128)(2,1)} %gather_levels.1) | copy-start | bytes 9437188

commit v3 on v2

--- a/solution.py
+++ b/solution.py
@@ -57,8 +57,15 @@
 
     pl.semaphore_wait(barrier, n_off + jnp.where(has_up, 1, 0) + jnp.where(has_down, 1, 0))
 
+    def partner(step):
+        bit, total = 1, 0
+        while bit < n_off:
+            total = total + bit * lax.rem(lax.rem(lax.div(o, bit), 2) + lax.rem(lax.div(step, bit), 2), 2)
+            bit *= 2
+        return total
+
     def xy_copy(step):
-        p = (o + step) % n_off
+        p = partner(jnp.int32(step))
         return pltpu.make_async_remote_copy(
             src_ref=send.at[p], dst_ref=buf.at[i, o], send_sem=xy_sem.at[step], recv_sem=recv_sem.at[i, o],
             device_id=(p, i), device_id_type=MESH)
@@ -98,7 +105,7 @@
         out_copy(j, q).start()
 
     def first_chunk(step, carry):
-        q = lax.rem(o - step + n_off, n_off)
+        q = partner(step)
 
         @pl.when(step > 0)
         def _():
@@ -120,7 +127,7 @@
 
     def one_chunk(turn, carry):
         d = lax.div(turn, n_off) + 1
-        q = lax.rem(o - lax.rem(turn, n_off) + n_off, n_off)
+        q = partner(lax.rem(turn, n_off))
         below = i - 2 * d
         above = i + 2 * d
         from_below = z >= d
@@ -262,7 +269,7 @@
             num_scalar_prefetch=2,
             grid=(blocks,),
             in_specs=[
-                pl.BlockSpec(memory_space=pl.ANY),
+                pl.BlockSpec(memory_space=pltpu.HBM),
                 pl.BlockSpec((CB, rows), lambda b, *_: (b, 0)),
             ],
             out_specs=pl.BlockSpec((CB, NT), lambda b, *_: (b, 0)),

time: 30.8 us -> 30.2 us (0.981)
  Pallas kernels: 28.7 us -> 28.1 us
    pallas_call x1, Pallas kernels: 24.8 us -> 24.2 us  [gather_levels(): pl.pallas_call(functools.partial(gather_kernel, n_off, n_img), out_shape=...]
where the time goes in v3:
time: 30.2 us; the launch traced here: 30 us
  Pallas kernels  28.1 us (93%)
  local copies, waits for them, and re-layouts  1.89 us (6%)
    pallas_call x1, Pallas kernels, gather_levels(): pl.pallas_call(functools.partial(gather_kernel, n_off, n_img), out_shape=...  24.2 us
    pallas_call x1, Pallas kernels, migrate(): pl.pallas_call(migrate_kernel, out_shape=jax.ShapeDtypeStruct((columns, N...  3.86 us
    unnamed x8, local copies, waits for them, and re-layouts  1.89 us

profile of v3, /device:TPU:0, one launch (start us, length us, event | category | flops | bytes accessed | tf_op | source)
XLA Modules:
  0.0 30.0 jit_solution(10625603274731750321)
XLA Ops:
  0.0 0.0 copy-start.3
  0.0 0.0 copy-start.2
  0.0 0.0 copy-start.1
  0.0 24.2 %gather_levels.1 = bf16[2,8,4,8,3072]{4,3,2,1,0:T(8,128)(2,1)} custom-call(bf16[32,3072]{1,0:T(8,128)(2,1)} %traces_hbm.1, s32[1,32]{1,0:T(1,128)} %bitcast.11, s32[1,32]{1,0:T(1,128)} %bitcast.12), custom_call_target="tpu_custom_call" | custom-call | tf_op jit(solution)/shard_map/gather_levels/pallas_call | solution.py:210
  24.2 0.0 copy-done.3
  24.2 0.0 copy-done.2
  24.3 0.0 copy-done.1
  24.3 0.0 copy-start
  24.3 1.9 %copy-done = bf16[2,8,4,8,3072]{4,3,2,1,0:T(8,128)(2,1)S(1)} copy-done((bf16[2,8,4,8,3072]{4,3,2,1,0:T(8,128)(2,1)S(1)}, bf16[2,8,4,8,3072]{4,3,2,1,0:T(8,128)(2,1)}, u32[]{:S(2)}) %copy-start) | copy-done | bytes 3145752
  26.2 3.9 %migrate.1 = bf16[512,1536]{1,0:T(8,128)(2,1)} custom-call(s32[4]{0:T(128)S(1)} %bitcast.9, s32[4]{0:T(128)S(1)} %bitcast.10, bf16[2,256,3072]{2,1,0:T(8,128)(2,1)S(1)} %bitcast.7, bf16[512,256]{1,0:T(8,128)(2,1)S(1)} %bitcast.8), custom_call_target="tpu_custom_call" | custom-call | tf_op jit(solution)/shard_map/migrate/pallas_call | solution.py:265
Async XLA Ops:
  0.0 24.2 %copy-start.3 = (s32[1,4]{1,0:T(1,128)S(1)}, s32[1,4]{1,0:T(1,128)}, u32[]{:S(2)}) copy-start(s32[1,4]{1,0:T(1,128)} %param.11) | copy-start | bytes 52
  0.0 24.2 %copy-start.2 = (s32[1,4]{1,0:T(1,128)S(1)}, s32[1,4]{1,0:T(1,128)}, u32[]{:S(2)}) copy-start(s32[1,4]{1,0:T(1,128)} %param.10) | copy-start | bytes 52
  0.0 24.2 %copy-start.1 = (bf16[1,512,256]{2,1,0:T(8,128)(2,1)S(1)}, bf16[1,512,256]{2,1,0:T(8,128)(2,1)}, u32[]{:S(2)}) copy-start(bf16[1,512,256]{2,1,0:T(8,128)(2,1)} %param.9) | copy-start | bytes 786436
  24.3 1.9 %copy-start = (bf16[2,8,4,8,3072]{4,3,2,1,0:T(8,128)(2,1)S(1)}, bf16[2,8,4,8,3072]{4,3,2,1,0:T(8,128)(2,1)}, u32[]{:S(2)}) copy-start(bf16[2,8,4,8,3072]{4,3,2,1,0:T(8,128)(2,1)} %gather_levels.1) | copy-start | bytes 9437188

commit v4 on v3

--- a/solution.py
+++ b/solution.py
@@ -278,7 +278,7 @@
                 pltpu.SemaphoreType.DMA((blocks,)),
             ],
         ),
-        compiler_params=pltpu.CompilerParams(vmem_limit_bytes=48 * 1024 * 1024),
+        compiler_params=pltpu.CompilerParams(vmem_limit_bytes=62 * 1024 * 1024),
         name="migrate",
     )(band_rows, smooth_rows, levels, weight_rows)
 

time: 30.2 us -> 30.4 us (level)
  Pallas kernels: 28.1 us -> 30.1 us
  local copies, waits for them, and re-layouts: 1.89 us -> 0 us
    pallas_call x1, Pallas kernels: 3.86 us -> 6.01 us  [migrate(): pl.pallas_call(migrate_kernel, out_shape=jax.ShapeDtypeStruct((columns, N...]
    unnamed x8 -> x0, local copies, waits for them, and re-layouts: 1.89 us -> none
where the time goes in v4:
time: 30.4 us; the launch traced here: 30.1 us
  Pallas kernels  30.1 us (99%)
    pallas_call x1, Pallas kernels, gather_levels(): pl.pallas_call(functools.partial(gather_kernel, n_off, n_img), out_shape=...  24.1 us
    pallas_call x1, Pallas kernels, migrate(): pl.pallas_call(migrate_kernel, out_shape=jax.ShapeDtypeStruct((columns, N...  6.01 us

profile of v4, /device:TPU:0, one launch (start us, length us, event | category | flops | bytes accessed | tf_op | source)
XLA Modules:
  0.0 30.1 jit_solution(3510517429242368559)
XLA Ops:
  0.0 24.1 %gather_levels.1 = bf16[2,8,4,8,3072]{4,3,2,1,0:T(8,128)(2,1)} custom-call(bf16[32,3072]{1,0:T(8,128)(2,1)} %traces_hbm.1, s32[1,32]{1,0:T(1,128)} %bitcast.9, s32[1,32]{1,0:T(1,128)} %bitcast.10), custom_call_target="tpu_custom_call" | custom-call | tf_op jit(solution)/shard_map/gather_levels/pallas_call | solution.py:210
  24.1 6.0 %migrate.1 = bf16[512,1536]{1,0:T(8,128)(2,1)} custom-call(s32[4]{0:T(128)} %bitcast.11, s32[4]{0:T(128)} %bitcast.12, bf16[2,256,3072]{2,1,0:T(8,128)(2,1)} %bitcast.7, bf16[512,256]{1,0:T(8,128)(2,1)} %bitcast.8), custom_call_target="tpu_custom_call" | custom-call | tf_op jit(solution)/shard_map/migrate/pallas_call | solution.py:265

commit v5 on v4

--- a/solution.py
+++ b/solution.py
@@ -209,7 +209,7 @@
     hbm = pl.BlockSpec(memory_space=pl.ANY)
     return pl.pallas_call(
         functools.partial(gather_kernel, n_off, n_img),
-        out_shape=jax.ShapeDtypeStruct((2, n_img, n_off, per, samples), jnp.bfloat16),
+        out_shape=pltpu.VMEM((2, n_img, n_off, per, samples), jnp.bfloat16),
         in_specs=[hbm] * 3,
         out_specs=hbm,
         scratch_shapes=[
@@ -228,32 +228,20 @@
             pltpu.SemaphoreType.DMA((n_img, n_off)),
         ],
         compiler_params=pltpu.CompilerParams(
-            collective_id=0, has_side_effects=True, vmem_limit_bytes=56 * 1024 * 1024),
+            collective_id=0, has_side_effects=True,
+            vmem_limit_bytes=60 * 1024 * 1024 - 4 * n_img * rows * samples),
         name="gather_levels",
     )(traces, offset_bins.reshape(1, rows), class_slots.reshape(1, rows))
 
 
-def migrate_kernel(band_ref, smooth_ref, levels, weights_ref, out_ref, segments, sems):
+def migrate_kernel(band_ref, smooth_ref, levels, weights_ref, out_ref):
     samples = levels.shape[2]
-    span = segments.shape[2]
-    blocks = segments.shape[0]
+    span = NT + 128
     block = pl.program_id(0)
-
-    def base_of(b):
-        return jnp.minimum(lax.div(band_ref[b], 128), (samples - span) // 128) * 128
-
-    def segment_copy(b):
-        band = pl.ds(pl.multiple_of(base_of(b), 128), span)
-        return pltpu.make_async_copy(levels.at[smooth_ref[b], :, band], segments.at[b], sems.at[b])
-
-    @pl.when(block == 0)
-    def _():
-        for b in range(blocks):
-            segment_copy(b).start()
-
-    segment_copy(block).wait()
-    shift = band_ref[block] - base_of(block)
-    product = jnp.dot(weights_ref[...], segments[block], preferred_element_type=jnp.float32)
+    base = jnp.minimum(lax.div(band_ref[block], 128), (samples - span) // 128) * 128
+    shift = band_ref[block] - base
+    segment = levels[smooth_ref[block], :, pl.ds(pl.multiple_of(base, 128), span)]
+    product = jnp.dot(weights_ref[...], segment, preferred_element_type=jnp.float32)
     turned = pltpu.roll(product, lax.rem(span - shift, span), 1)
     out_ref[...] = turned[:, :NT].astype(jnp.bfloat16)
 
@@ -261,24 +249,19 @@
 def migrate(levels, weight_rows, band_rows, smooth_rows):
     rows = levels.shape[1]
     columns = weight_rows.shape[0]
-    blocks = columns // CB
     return pl.pallas_call(
         migrate_kernel,
         out_shape=jax.ShapeDtypeStruct((columns, NT), jnp.bfloat16),
         grid_spec=pltpu.PrefetchScalarGridSpec(
             num_scalar_prefetch=2,
-            grid=(blocks,),
+            grid=(columns // CB,),
             in_specs=[
-                pl.BlockSpec(memory_space=pltpu.HBM),
+                pl.BlockSpec(memory_space=pltpu.VMEM),
                 pl.BlockSpec((CB, rows), lambda b, *_: (b, 0)),
             ],
             out_specs=pl.BlockSpec((CB, NT), lambda b, *_: (b, 0)),
-            scratch_shapes=[
-                pltpu.VMEM((blocks, rows, NT + 128), jnp.bfloat16),
-                pltpu.SemaphoreType.DMA((blocks,)),
-            ],
         ),
-        compiler_params=pltpu.CompilerParams(vmem_limit_bytes=62 * 1024 * 1024),
+        compiler_params=pltpu.CompilerParams(vmem_limit_bytes=40 * 1024 * 1024),
         name="migrate",
     )(band_rows, smooth_rows, levels, weight_rows)
 

time: 30.4 us -> 28.5 us (0.938)
  Pallas kernels: 30.1 us -> 28.3 us
    pallas_call x1, Pallas kernels: 6.01 us -> 3.53 us  [migrate(): pl.pallas_call(migrate_kernel, out_shape=jax.ShapeDtypeStruct((columns, N...]
    pallas_call x1, Pallas kernels: 24.1 us -> 24.7 us  [gather_levels(): pl.pallas_call(functools.partial(gather_kernel, n_off, n_img), out_shape=...]
where the time goes in v5:
time: 28.5 us; the launch traced here: 28.3 us
  Pallas kernels  28.3 us (99%)
    pallas_call x1, Pallas kernels, gather_levels(): pl.pallas_call(functools.partial(gather_kernel, n_off, n_img), out_shape=...  24.7 us
    pallas_call x1, Pallas kernels, migrate(): pl.pallas_call(migrate_kernel, out_shape=jax.ShapeDtypeStruct((columns, N...  3.53 us

profile of v5, /device:TPU:0, one launch (start us, length us, event | category | flops | bytes accessed | tf_op | source)
XLA Modules:
  0.0 28.3 jit_solution(12908817008683995242)
XLA Ops:
  0.0 0.0 copy-start.2
  0.0 0.0 copy-start.1
  0.0 0.0 copy-start
  0.0 24.7 %gather_levels.1 = bf16[2,8,4,8,3072]{4,3,2,1,0:T(8,128)(2,1)S(1)} custom-call(bf16[32,3072]{1,0:T(8,128)(2,1)} %traces_hbm.1, s32[1,32]{1,0:T(1,128)} %bitcast.11, s32[1,32]{1,0:T(1,128)} %bitcast.12), custom_call_target="tpu_custom_call" | custom-call | tf_op jit(solution)/shard_map/gather_levels/pallas_call | solution.py:210
  24.8 0.0 copy-done.2
  24.8 0.0 copy-done.1
  24.8 0.0 copy-done
  24.8 3.5 %migrate.1 = bf16[512,1536]{1,0:T(8,128)(2,1)} custom-call(s32[4]{0:T(128)S(1)} %bitcast.9, s32[4]{0:T(128)S(1)} %bitcast.10, bf16[2,256,3072]{2,1,0:T(8,128)(2,1)S(1)} %bitcast.7, bf16[512,256]{1,0:T(8,128)(2,1)S(1)} %bitcast.8), custom_call_target="tpu_custom_call" | custom-call | tf_op jit(solution)/shard_map/migrate/pallas_call | solution.py:252
Async XLA Ops:
  0.0 24.8 %copy-start.2 = (s32[1,4]{1,0:T(1,128)S(1)}, s32[1,4]{1,0:T(1,128)}, u32[]{:S(2)}) copy-start(s32[1,4]{1,0:T(1,128)} %param.11) | copy-start | bytes 52
  0.0 24.8 %copy-start.1 = (s32[1,4]{1,0:T(1,128)S(1)}, s32[1,4]{1,0:T(1,128)}, u32[]{:S(2)}) copy-start(s32[1,4]{1,0:T(1,128)} %param.10) | copy-start | bytes 52
  0.0 24.8 %copy-start = (bf16[1,512,256]{2,1,0:T(8,128)(2,1)S(1)}, bf16[1,512,256]{2,1,0:T(8,128)(2,1)}, u32[]{:S(2)}) copy-start(bf16[1,512,256]{2,1,0:T(8,128)(2,1)} %param.9) | copy-start | bytes 786436

commit v6 on v5

--- a/solution.py
+++ b/solution.py
@@ -12,8 +12,8 @@
 MESH = pl.DeviceIdType.MESH
 
 
-def gather_kernel(n_off, n_img, traces_hbm, bins_hbm, slots_hbm, out, traces_ref, bins_ref, slots_ref, buf, levels, send,
-                  in_sem, xy_sem, up_sem, down_sem, sib_sem, recv_sem, out_sem):
+def gather_kernel(n_off, n_img, traces_hbm, bins_hbm, slots_hbm, levels, traces_ref, bins_ref, slots_ref, buf, send,
+                  in_sem, xy_sem, up_sem, down_sem, sib_sem, recv_sem):
     o = lax.axis_index("off")
     i = lax.axis_index("img")
     rows = traces_ref.shape[0]
@@ -82,9 +82,6 @@
 
     for step in range(1, n_off):
         xy_copy(step).start()
-
-    def out_copy(j, q):
-        return pltpu.make_async_copy(levels.at[:, j, q], out.at[:, j, q], out_sem.at[j, q])
 
     def filter_chunk(j, q):
         samples = buf.shape[3]
@@ -102,7 +99,6 @@
         ) / 9.0
         levels[0, j, q] = boosted.astype(jnp.bfloat16)
         levels[1, j, q] = smoothed[:, :samples].astype(jnp.bfloat16)
-        out_copy(j, q).start()
 
     def first_chunk(step, carry):
         q = partner(step)
@@ -181,8 +177,6 @@
 
         def last(q, carry):
             mine = 2 * w + core
-            out_copy(2 * w, q).wait()
-            out_copy(2 * w + 1, q).wait()
             chunk_copy(mine, q, sib_sem, sibling).wait_send()
 
             @pl.when(jnp.logical_and(has_up, w <= z))
@@ -211,17 +205,15 @@
         functools.partial(gather_kernel, n_off, n_img),
         out_shape=pltpu.VMEM((2, n_img, n_off, per, samples), jnp.bfloat16),
         in_specs=[hbm] * 3,
-        out_specs=hbm,
+        out_specs=pl.BlockSpec(memory_space=pltpu.VMEM),
         scratch_shapes=[
             pltpu.VMEM((rows, samples), jnp.bfloat16),
             pltpu.VMEM((1, rows), jnp.int32),
             pltpu.VMEM((1, rows), jnp.int32),
             pltpu.VMEM((n_img, n_off, per, samples), jnp.bfloat16),
-            pltpu.VMEM((2, n_img, n_off, per, samples), jnp.bfloat16),
             pltpu.VMEM((n_off, per, samples), jnp.bfloat16),
             pltpu.SemaphoreType.DMA((3,)),
             pltpu.SemaphoreType.DMA((n_off,)),
-            pltpu.SemaphoreType.DMA((n_img, n_off)),
             pltpu.SemaphoreType.DMA((n_img, n_off)),
             pltpu.SemaphoreType.DMA((n_img, n_off)),
             pltpu.SemaphoreType.DMA((n_img, n_off)),

time: 28.5 us -> 27.2 us (0.954)
  Pallas kernels: 28.3 us -> 27 us
    pallas_call x1, Pallas kernels: 24.7 us -> 23.5 us  [gather_levels(): pl.pallas_call(functools.partial(gather_kernel, n_off, n_img), out_shape=...]
where the time goes in v6:
time: 27.2 us; the launch traced here: 27 us
  Pallas kernels  27 us (99%)
    pallas_call x1, Pallas kernels, gather_levels(): pl.pallas_call(functools.partial(gather_kernel, n_off, n_img), out_shape=...  23.5 us
    pallas_call x1, Pallas kernels, migrate(): pl.pallas_call(migrate_kernel, out_shape=jax.ShapeDtypeStruct((columns, N...  3.53 us

profile of v6, /device:TPU:0, one launch (start us, length us, event | category | flops | bytes accessed | tf_op | source)
XLA Modules:
  0.0 27.0 jit_solution(17556787135932586667)
XLA Ops:
  0.0 0.0 copy-start.2
  0.0 0.0 copy-start.1
  0.0 0.0 copy-start
  0.0 23.5 %gather_levels.1 = bf16[2,8,4,8,3072]{4,3,2,1,0:T(8,128)(2,1)S(1)} custom-call(bf16[32,3072]{1,0:T(8,128)(2,1)} %traces_hbm.1, s32[1,32]{1,0:T(1,128)} %bitcast.11, s32[1,32]{1,0:T(1,128)} %bitcast.12), custom_call_target="tpu_custom_call" | custom-call | tf_op jit(solution)/shard_map/gather_levels/pallas_call | solution.py:204
  23.5 0.0 copy-done.2
  23.5 0.0 copy-done.1
  23.5 0.0 copy-done
  23.5 3.5 %migrate.1 = bf16[512,1536]{1,0:T(8,128)(2,1)} custom-call(s32[4]{0:T(128)S(1)} %bitcast.9, s32[4]{0:T(128)S(1)} %bitcast.10, bf16[2,256,3072]{2,1,0:T(8,128)(2,1)S(1)} %bitcast.7, bf16[512,256]{1,0:T(8,128)(2,1)S(1)} %bitcast.8), custom_call_target="tpu_custom_call" | custom-call | tf_op jit(solution)/shard_map/migrate/pallas_call | solution.py:244
Async XLA Ops:
  0.0 23.5 %copy-start.2 = (s32[1,4]{1,0:T(1,128)S(1)}, s32[1,4]{1,0:T(1,128)}, u32[]{:S(2)}) copy-start(s32[1,4]{1,0:T(1,128)} %param.11) | copy-start | bytes 52
  0.0 23.5 %copy-start.1 = (s32[1,4]{1,0:T(1,128)S(1)}, s32[1,4]{1,0:T(1,128)}, u32[]{:S(2)}) copy-start(s32[1,4]{1,0:T(1,128)} %param.10) | copy-start | bytes 52
  0.0 23.5 %copy-start = (bf16[1,512,256]{2,1,0:T(8,128)(2,1)S(1)}, bf16[1,512,256]{2,1,0:T(8,128)(2,1)}, u32[]{:S(2)}) copy-start(bf16[1,512,256]{2,1,0:T(8,128)(2,1)} %param.9) | copy-start | bytes 786436
